TPU v7x, 32 devices: a whole 2x2x4 slice. The times are simulated.
32 devices in a mesh: grp: 2 (over x), area: 8 (over z, y), ctg: 2 (over core).
Axes of the slice: x: 2, y: 2, z: 4, core: 2. Of those that a mesh axis runs over, the one named last changes fastest.
Arguments:
- area_size: int32 [16], P(('grp', 'area')), parts along dimension 0, may hold values from 299 to 1024, as said below
- tie_peer: int32 [16, 42], P(('grp', 'area')), parts along dimension 0, may hold values from 0 to 7, as said below
- kkt_diag: float32 [16, 2, 1024], P(('grp', 'area'), 'ctg'), parts along dimension 0, may hold values from 0.5 to 1
- kkt_offdiag: float32 [16, 2, 1024, 1024], P(('grp', 'area'), 'ctg'), parts along dimension 0, may hold values from -0.1875 to 0.1875
- cost: float32 [16, 2, 1024, 256], P(('grp', 'area'), 'ctg'), parts along dimension 0, may hold values from -6 to 6
- consensus: float32 [16, 2, 1024, 256], P(('grp', 'area'), 'ctg'), parts along dimension 0, may hold values from -4 to 4
- dual: float32 [16, 2, 1024, 256], P(('grp', 'area'), 'ctg'), parts along dimension 0, may hold values from -4 to 4
- limit: float32 [16, 1024, 256], P(('grp', 'area')), parts along dimension 0, may hold values from 0.3 to 1.5
Outputs:
- agreed_out: float32 [16, 2, 1024, 256], P(('grp', 'area'), 'ctg'), parts along dimension 0
- dual_out: float32 [16, 2, 1024, 256], P(('grp', 'area'), 'ctg'), parts along dimension 0
There are 2 independent parts, one for each index of `grp`. A program takes and returns all parts, laid end to end along the dimension named above; each array names one. Nothing has to cross between parts.
Inputs may be any that keep to these rules, and one draw needn't show every extreme that they name: `area_size`: some area has exactly 1024 live slots. `tie_peer`: never the area itself; each area has exactly 6 tie slots to each other area.
All inputs are finite; a program needn't handle non-finite values.
Results may differ from a plain program's by a relative error of at most 0.0003.
Values sent between devices are 32-bit elements; how exact they have to be, the bound alone decides.
A program may use at most 64 MiB of HBM per device.

v0:
```python
import jax
import jax.numpy as jnp
from jax import lax
from jax.sharding import PartitionSpec as P

GENS = 256
ITERS = 3


def tie_dest(peers, pair_lines):
    count = peers.shape[0]
    order = jnp.arange(count)
    same = (peers[:, None] == peers[None, :]) & (order[:, None] < order[None, :])
    rank = jnp.sum(same.astype(jnp.int32), axis=0)
    return peers * pair_lines + rank


def apply_rows(matrix, right_side):
    return jnp.dot(
        matrix, right_side, precision=lax.Precision.HIGHEST, preferred_element_type=jnp.float32
    )


def local(area_size, tie_peer, kkt_diag, kkt_offdiag, cost, consensus, dual, limit):
    areas = lax.axis_size("area")
    scenarios = lax.axis_size("ctg")
    peers = tie_peer[0]
    ties = peers.shape[0]
    pair_lines = ties // (areas - 1)
    dest = tie_dest(peers, pair_lines)
    slots = cost.shape[2]
    hours = cost.shape[3]
    shared = GENS + ties
    live = (jnp.arange(slots) < area_size[0]).astype(jnp.float32)[:, None]
    offdiag = kkt_offdiag[0, 0]
    diagonal = kkt_diag[0, 0][:, None]
    bound = limit[0]
    linear = cost[0, 0]
    agreed = consensus[0, 0]
    dual_var = dual[0, 0]
    for iteration in range(ITERS):
        right_side = live * (agreed - dual_var - linear)
        primal = live * (diagonal * right_side + apply_rows(offdiag, right_side))
        primal_top = primal[:shared]
        dual_top = dual_var[:shared]
        shifted = primal_top + dual_top
        gen_mean = lax.psum(shifted[:GENS], "ctg") / scenarios
        empty = jnp.zeros((areas * pair_lines, hours), jnp.float32)
        sent_primal = empty.at[dest].set(primal_top[GENS:])
        sent_dual = empty.at[dest].set(dual_top[GENS:])
        got_primal = lax.all_to_all(sent_primal, "area", split_axis=0, concat_axis=0, tiled=True)
        got_dual = lax.all_to_all(sent_dual, "area", split_axis=0, concat_axis=0, tiled=True)
        other = got_primal[dest] + got_dual[dest]
        top_part = jnp.concatenate([gen_mean, 0.5 * (shifted[GENS:] + other)], axis=0)
        averaged = jnp.concatenate([top_part, primal[shared:] + dual_var[shared:]], axis=0)
        agreed = live * jnp.clip(averaged, -bound, bound)
        dual_var = live * (dual_var + primal - agreed)
    return (agreed[None, None], dual_var[None, None])


def solution(mesh):
    return jax.shard_map(
        local,
        mesh=mesh,
        in_specs=(
            P(("grp", "area")),
            P(("grp", "area"), None),
            P(("grp", "area"), "ctg", None),
            P(("grp", "area"), "ctg", None, None),
            P(("grp", "area"), "ctg", None, None),
            P(("grp", "area"), "ctg", None, None),
            P(("grp", "area"), "ctg", None, None),
            P(("grp", "area"), None, None),
        ),
        out_specs=(P(("grp", "area"), "ctg", None, None), P(("grp", "area"), "ctg", None, None)),
        check_vma=False,
    )
```

profile of v0, /device:TPU:0, one launch (start us, length us, event | category | flops | bytes accessed | tf_op | source)
XLA Modules:
  0.0 138.7 jit_solution(8805056950843362891)
XLA Ops:
  10.3 7.3 %all-to-all-start.1 = ((f32[8,6,256]{2,1,0:T(8,128)}), f32[8,6,256]{2,1,0:T(8,128)S(1)}, u32[]{:S(2)}, u32[]{:S(2)}) async-start(f32[8,6,256]{2,1,0:T(8,128)} %all_to_all.51), calls=%async_computation.1 | async-start | bytes 131072 | tf_op jit(solution)/shard_map/all_to_all | solution.py:52
  18.3 7.7 %fusion.12 = f32[1024,256]{1,0:T(8,128)S(1)} fusion(f32[1,1,1024,1024]{3,2,1,0:T(8,128)} %param.11, f32[1,1,1024,256]{3,2,1,0:T(8,128)} %param.12, f32[1,1,1024,256]{3,2,1,0:T(8,128)} %param.14, f32[1,1,1024,256]{3,2,1,0:T(8,128)} %param.13, f32[1024]{0:T(1024)} %bitcast.144, f32[1024]{0:T(1024)S(1)} %fusion.84), kind=kOutput, calls=%fused_computation.20 | convolution fusion | flops 3223584768 | bytes 8396800 | tf_op jit(solution)/shard_map/dot_general | solution.py:19
  27.7 1.3 slice_add_fusion.2
  30.7 6.0 %all-to-all-start = ((f32[8,6,256]{2,1,0:T(8,128)}), f32[8,6,256]{2,1,0:T(8,128)S(1)}, u32[]{:S(2)}, u32[]{:S(2)}) async-start(f32[8,6,256]{2,1,0:T(8,128)} %all_to_all.48), calls=%async_computation | async-start | bytes 131072 | tf_op jit(solution)/shard_map/all_to_all | solution.py:51
  37.3 6.3 %all-to-all-done = f32[8,6,256]{2,1,0:T(8,128)S(1)} async-done(((f32[8,6,256]{2,1,0:T(8,128)}), f32[8,6,256]{2,1,0:T(8,128)S(1)}, u32[]{:S(2)}, u32[]{:S(2)}) %all-to-all-start) | async-done | bytes 49184 | tf_op jit(solution)/shard_map/all_to_all | solution.py:51
  44.2 3.3 %all-reduce.4.cloned.1.call-done = f32[256,256]{1,0:T(8,128)} async-done(((f32[256,256]{1,0:T(8,128)}), f32[256,256]{1,0:T(8,128)}) %all-reduce.4.cloned.1.call-update) | async-done | bytes 262160 | tf_op jit(solution)/shard_map/psum | solution.py:47
  48.7 2.1 %fusion.50 = f32[1024,256]{1,0:T(8,128)S(1)} fusion(f32[1024,256]{1,0:T(8,128)} %copy-done.5, f32[1,1,1024,256]{3,2,1,0:T(8,128)} %param.14, f32[1024]{0:T(1024)S(1)} %fusion.84, f32[726,256]{1,0:T(8,128)S(1)} %slice_add_fusion.2, f32[42,256]{1,0:T(8,128)S(1)} %fusion.73, f32[256,256]{1,0:T(8,128)S(1)} %broadcast_multiply_fusion.2, ...), kind=kLoop, calls=%fused_computation.53 | loop fusion | flops 2359296 | bytes 5246976 | tf_op jit(solution)/shard_map/mul | solution.py:57
  50.8 6.5 %fusion.21 = f32[1024,256]{1,0:T(8,128)} fusion(f32[1,1,1024,1024]{3,2,1,0:T(8,128)S(1)} %copy-done, f32[1,1,1024,256]{3,2,1,0:T(8,128)} %param.12, f32[1024,256]{1,0:T(8,128)S(1)} %fusion.50, f32[1024]{0:T(1024)S(1)} %bitcast.145, f32[1024]{0:T(1024)S(1)} %fusion.84, f32[726,256]{1,0:T(8,128)S(1)} %slice_add_fusion.2, f32[42,256]{1,0:T(8,128)S(1)} %fusion.73, ...), kind=kOutput, calls=%fused_computation.23 | convolution fusion | flops 3226730496 | bytes 9445376 | tf_op jit(solution)/shard_map/dot_general | solution.py:19
  59.0 5.8 %all-to-all-start.2 = ((f32[8,6,256]{2,1,0:T(8,128)}), f32[8,6,256]{2,1,0:T(8,128)S(1)}, u32[]{:S(2)}, u32[]{:S(2)}) async-start(f32[8,6,256]{2,1,0:T(8,128)} %all_to_all.54), calls=%async_computation.2 | async-start | bytes 131072 | tf_op jit(solution)/shard_map/all_to_all | solution.py:51
  68.0 3.7 %all-to-all-done.2 = f32[8,6,256]{2,1,0:T(8,128)S(1)} async-done(((f32[8,6,256]{2,1,0:T(8,128)}), f32[8,6,256]{2,1,0:T(8,128)S(1)}, u32[]{:S(2)}, u32[]{:S(2)}) %all-to-all-start.2) | async-done | bytes 49184 | tf_op jit(solution)/shard_map/all_to_all | solution.py:51
  71.7 3.5 %all-to-all-start.3 = ((f32[8,6,256]{2,1,0:T(8,128)}), f32[8,6,256]{2,1,0:T(8,128)S(1)}, u32[]{:S(2)}, u32[]{:S(2)}) async-start(f32[8,6,256]{2,1,0:T(8,128)} %all_to_all.57), calls=%async_computation.3 | async-start | bytes 131072 | tf_op jit(solution)/shard_map/all_to_all | solution.py:52
  75.2 2.1 %slice_add_fusion.1 = f32[726,256]{1,0:T(8,128)} fusion(f32[1024,256]{1,0:T(8,128)S(1)} %fusion.50, f32[1024,256]{1,0:T(8,128)} %fusion.21), kind=kLoop, calls=%fused_computation.63 | loop fusion | flops 185856 | bytes 2230272 | tf_op jit(solution)/shard_map/add | solution.py:55
  78.0 3.9 %all-to-all-done.3 = f32[8,6,256]{2,1,0:T(8,128)S(1)} async-done(((f32[8,6,256]{2,1,0:T(8,128)}), f32[8,6,256]{2,1,0:T(8,128)S(1)}, u32[]{:S(2)}, u32[]{:S(2)}) %all-to-all-start.3) | async-done | bytes 49184 | tf_op jit(solution)/shard_map/all_to_all | solution.py:52
  82.6 5.2 %all-reduce.6.cloned.1.call-done = f32[256,256]{1,0:T(8,128)} async-done(((f32[256,256]{1,0:T(8,128)}), f32[256,256]{1,0:T(8,128)}) %all-reduce.6.cloned.1.call-update) | async-done | bytes 262160 | tf_op jit(solution)/shard_map/psum | solution.py:47
  88.9 2.3 %subtract_multiply_fusion = f32[1024,256]{1,0:T(8,128)S(1)} fusion(f32[1024,256]{1,0:T(8,128)S(1)} %fusion.50, f32[1024,256]{1,0:T(8,128)} %fusion.21, f32[1024]{0:T(1024)S(1)} %fusion.84, f32[726,256]{1,0:T(8,128)} %slice_add_fusion.1, f32[42,256]{1,0:T(8,128)S(1)} %fusion.70, f32[256,256]{1,0:T(8,128)S(1)} %broadcast_multiply_fusion.1, ...), kind=kLoop, calls=%fused_computation.57 | loop fusion | flops 2359296 | bytes 5246976 | tf_op jit(solution)/shard_map/mul | solution.py:57
  91.2 5.6 %fusion.30 = f32[1024,256]{1,0:T(8,128)S(1)} fusion(f32[1,1,1024,1024]{3,2,1,0:T(8,128)S(1)} %copy-done.1, f32[1,1,1024,256]{3,2,1,0:T(8,128)} %param.12, f32[1024,256]{1,0:T(8,128)S(1)} %subtract_multiply_fusion, f32[1024]{0:T(1024)S(1)} %bitcast.146, f32[1024]{0:T(1024)S(1)} %fusion.84, f32[726,256]{1,0:T(8,128)S(1)} %copy-done.3, ...), kind=kOutput, calls=%fused_computation.26 | convolution fusion | flops 3226730496 | bytes 9445376 | tf_op jit(solution)/shard_map/dot_general | solution.py:19
  98.2 5.8 %all-to-all-start.4 = ((f32[8,6,256]{2,1,0:T(8,128)}), f32[8,6,256]{2,1,0:T(8,128)}, u32[]{:S(2)}, u32[]{:S(2)}) async-start(f32[8,6,256]{2,1,0:T(8,128)} %all_to_all.60), calls=%async_computation.4 | async-start | bytes 131072 | tf_op jit(solution)/shard_map/all_to_all | solution.py:51
  106.2 4.8 %all-to-all-done.4 = f32[8,6,256]{2,1,0:T(8,128)} async-done(((f32[8,6,256]{2,1,0:T(8,128)}), f32[8,6,256]{2,1,0:T(8,128)}, u32[]{:S(2)}, u32[]{:S(2)}) %all-to-all-start.4) | async-done | bytes 49184 | tf_op jit(solution)/shard_map/all_to_all | solution.py:51
  111.0 4.0 %all-to-all-start.5 = ((f32[8,6,256]{2,1,0:T(8,128)}), f32[8,6,256]{2,1,0:T(8,128)}, u32[]{:S(2)}, u32[]{:S(2)}) async-start(f32[8,6,256]{2,1,0:T(8,128)} %all_to_all.63), calls=%async_computation.5 | async-start | bytes 131072 | tf_op jit(solution)/shard_map/all_to_all | solution.py:52
  116.8 1.2 gather_fusion.4
  118.0 3.9 %all-to-all-done.5 = f32[8,6,256]{2,1,0:T(8,128)} async-done(((f32[8,6,256]{2,1,0:T(8,128)}), f32[8,6,256]{2,1,0:T(8,128)}, u32[]{:S(2)}, u32[]{:S(2)}) %all-to-all-start.5) | async-done | bytes 49184 | tf_op jit(solution)/shard_map/all_to_all | solution.py:52
  124.8 2.6 %all-reduce.8.cloned.1.call-done = f32[256,256]{1,0:T(8,128)} async-done(((f32[256,256]{1,0:T(8,128)}), f32[256,256]{1,0:T(8,128)}) %all-reduce.8.cloned.1.call-update) | async-done | bytes 262160 | tf_op jit(solution)/shard_map/psum | solution.py:47
  128.4 2.5 %fusion.43 = f32[1,1,1024,256]{3,2,1,0:T(8,128)} fusion(f32[726,256]{1,0:T(8,128)} %slice_add_fusion, f32[42,256]{1,0:T(8,128)S(1)} %fusion.65, f32[256,256]{1,0:T(8,128)S(1)} %get-tuple-element.8, f32[1,1024,256]{2,1,0:T(8,128)S(1)} %copy-done.2, f32[1024,256]{1,0:T(8,128)S(1)} %subtract_multiply_fusion, f32[1024,256]{1,0:T(8,128)S(1)} %fusion.30, ...), kind=kLoop, calls=%fused_computation.41 | loop fusion | flops 2359296 | bytes 5246976 | tf_op jit(solution)/shard_map/broadcast_in_dim | solution.py:58
  130.9 1.3 fusion.38
  (63 shorter events, 25.5 us)
Async XLA Ops:
  10.3 20.4 %all-to-all-start.1 = ((f32[8,6,256]{2,1,0:T(8,128)}), f32[8,6,256]{2,1,0:T(8,128)S(1)}, u32[]{:S(2)}, u32[]{:S(2)}) async-start(f32[8,6,256]{2,1,0:T(8,128)} %all_to_all.51), calls=%async_computation.1 | async-start | bytes 131072 | tf_op jit(solution)/shard_map/all_to_all | solution.py:52
  17.6 30.0 %all-reduce.4.cloned.1.call-start = ((), (), s32[]{:S(2)}) async-start(), calls=%async_computation.6 | async-start | bytes 524288 | tf_op jit(solution)/shard_map/psum | solution.py:47
  18.3 8.7 %copy-start.4 = (f32[1,1,1024,256]{3,2,1,0:T(8,128)S(1)}, f32[1,1,1024,256]{3,2,1,0:T(8,128)}, u32[]{:S(2)}) copy-start(f32[1,1,1024,256]{3,2,1,0:T(8,128)} %param.14) | copy-start | bytes 3145732
  26.0 1.0 copy-start.5
  27.0 21.7 %copy-start.2 = (f32[1,1024,256]{2,1,0:T(8,128)S(1)}, f32[1,1024,256]{2,1,0:T(8,128)}, u32[]{:S(2)}) copy-start(f32[1,1024,256]{2,1,0:T(8,128)} %param.15) | copy-start | bytes 3145732
  29.1 21.8 %copy-start.7 = (f32[1,1,1024]{2,1,0:T(1,128)S(1)}, f32[1,1,1024]{2,1,0:T(1,128)}, u32[]{:S(2)}) copy-start(f32[1,1,1024]{2,1,0:T(1,128)} %param.10) | copy-start | bytes 12292
  30.7 12.9 %all-to-all-start = ((f32[8,6,256]{2,1,0:T(8,128)}), f32[8,6,256]{2,1,0:T(8,128)S(1)}, u32[]{:S(2)}, u32[]{:S(2)}) async-start(f32[8,6,256]{2,1,0:T(8,128)} %all_to_all.48), calls=%async_computation | async-start | bytes 131072 | tf_op jit(solution)/shard_map/all_to_all | solution.py:51
  47.5 3.3 %copy-start = (f32[1,1,1024,1024]{3,2,1,0:T(8,128)S(1)}, f32[1,1,1024,1024]{3,2,1,0:T(8,128)}, u32[]{:S(2)}) copy-start(f32[1,1,1024,1024]{3,2,1,0:T(8,128)} %param.11) | copy-start | bytes 12582916
  59.0 12.7 %all-to-all-start.2 = ((f32[8,6,256]{2,1,0:T(8,128)}), f32[8,6,256]{2,1,0:T(8,128)S(1)}, u32[]{:S(2)}, u32[]{:S(2)}) async-start(f32[8,6,256]{2,1,0:T(8,128)} %all_to_all.54), calls=%async_computation.2 | async-start | bytes 131072 | tf_op jit(solution)/shard_map/all_to_all | solution.py:51
  64.8 22.9 %all-reduce.6.cloned.1.call-start = ((), (), s32[]{:S(2)}) async-start(), calls=%async_computation.7 | async-start | bytes 524288 | tf_op jit(solution)/shard_map/psum | solution.py:47
  71.7 10.2 %all-to-all-start.3 = ((f32[8,6,256]{2,1,0:T(8,128)}), f32[8,6,256]{2,1,0:T(8,128)S(1)}, u32[]{:S(2)}, u32[]{:S(2)}) async-start(f32[8,6,256]{2,1,0:T(8,128)} %all_to_all.57), calls=%async_computation.3 | async-start | bytes 131072 | tf_op jit(solution)/shard_map/all_to_all | solution.py:52
  87.7 3.4 %copy-start.1 = (f32[1,1,1024,1024]{3,2,1,0:T(8,128)S(1)}, f32[1,1,1024,1024]{3,2,1,0:T(8,128)}, u32[]{:S(2)}) copy-start(f32[1,1,1024,1024]{3,2,1,0:T(8,128)} %param.11) | copy-start | bytes 12582916
  87.8 3.4 %copy-start.3 = (f32[726,256]{1,0:T(8,128)S(1)}, f32[726,256]{1,0:T(8,128)}, u32[]{:S(2)}) copy-start(f32[726,256]{1,0:T(8,128)} %slice_add_fusion.1) | copy-start | bytes 2230276
  98.2 12.8 %all-to-all-start.4 = ((f32[8,6,256]{2,1,0:T(8,128)}), f32[8,6,256]{2,1,0:T(8,128)}, u32[]{:S(2)}, u32[]{:S(2)}) async-start(f32[8,6,256]{2,1,0:T(8,128)} %all_to_all.60), calls=%async_computation.4 | async-start | bytes 131072 | tf_op jit(solution)/shard_map/all_to_all | solution.py:51
  103.9 23.4 %all-reduce.8.cloned.1.call-start = ((), (), s32[]{:S(2)}) async-start(), calls=%async_computation.8 | async-start | bytes 524288 | tf_op jit(solution)/shard_map/psum | solution.py:47
  111.0 10.9 %all-to-all-start.5 = ((f32[8,6,256]{2,1,0:T(8,128)}), f32[8,6,256]{2,1,0:T(8,128)}, u32[]{:S(2)}, u32[]{:S(2)}) async-start(f32[8,6,256]{2,1,0:T(8,128)} %all_to_all.63), calls=%async_computation.5 | async-start | bytes 131072 | tf_op jit(solution)/shard_map/all_to_all | solution.py:52
  127.4 3.5 %copy-start.6 = (f32[726,256]{1,0:T(8,128)S(1)}, f32[726,256]{1,0:T(8,128)}, u32[]{:S(2)}) copy-start(f32[726,256]{1,0:T(8,128)} %slice_add_fusion) | copy-start | bytes 2230276
Sparse Core Ops, SparseCore 0:
  27.9 19.6 all-reduce.3
  68.1 19.6 all-reduce.5
  107.7 19.6 all-reduce.7
where the time goes:
time: 140 us; the launch traced here: 139 us
  waiting for transfers between devices  33.7 us (24%)
  starting transfers between devices  32.4 us (23%)
  matrix products  19.8 us (14%)
  other arithmetic  19.3 us (14%)
  local copies, waits for them, and re-layouts  18.8 us (13%)
  between operations  14.6 us (10%)
    dot_general x3, matrix products, apply_rows(): jnp.dot(matrix, right_side, precision=lax.Precision.HIGHEST, preferred_el...  19.8 us
    all_to_all x3, starting transfers between devices, local(): lax.all_to_all(sent_primal, 'area', split_axis=0, concat_axis=0, tiled=True)  17.5 us
    all_to_all x3, waiting for transfers between devices, local(): lax.all_to_all(sent_primal, 'area', split_axis=0, concat_axis=0, tiled=True)  14.8 us
    all_to_all x3, starting transfers between devices, local(): lax.all_to_all(sent_dual, 'area', split_axis=0, concat_axis=0, tiled=True)  14.8 us
    psum x3, waiting for transfers between devices, local(): gen_mean = lax.psum(shifted[:GENS], 'ctg') / scenarios  11.1 us
    all_to_all x3, waiting for transfers between devices, local(): lax.all_to_all(sent_dual, 'area', split_axis=0, concat_axis=0, tiled=True)  7.78 us
    gather x6, local copies, waits for them, and re-layouts, local(): other = got_primal[dest] + got_dual[dest]  4.91 us
    mul x2, other arithmetic, local(): dual_var = live * (dual_var + primal - agreed)  4.41 us
  transfers between devices with their start and end apart: 9, of which 8 were waited for; matrix products, arithmetic and copies ran while one was open for 17% of the time, Pallas kernels for 0%

commit v1 on v0

v1 whole, which is shorter than its diff:
```python
import functools

import jax
import jax.numpy as jnp
from jax import lax
from jax.experimental import pallas as pl
from jax.experimental.pallas import tpu as pltpu
from jax.sharding import PartitionSpec as P

GENS = 256
ITERS = 3
MESH = pl.DeviceIdType.MESH


def round_up(value, step):
    return (value + step - 1) // step * step


def fast_dot(a, b):
    return jnp.dot(a, b, preferred_element_type=jnp.float32)


def split_two(x):
    high = x.astype(jnp.bfloat16)
    low = (x - high.astype(jnp.float32)).astype(jnp.bfloat16)
    return high, low


def move_rows(one_hot, x):
    width = x.shape[1]
    high = x.astype(jnp.bfloat16)
    rest = x - high.astype(jnp.float32)
    mid = rest.astype(jnp.bfloat16)
    low = (rest - mid.astype(jnp.float32)).astype(jnp.bfloat16)
    out = fast_dot(one_hot, jnp.concatenate([high, mid, low], axis=1))
    return out[:, :width] + out[:, width:2 * width] + out[:, 2 * width:]


def kernel(
    areas, scenarios, ties, size_ref, peer_ref, diag_ref, k_hbm, cost_hbm, cons_hbm, dual_hbm,
    limit_hbm, agreed_hbm, dualout_hbm,
    k_ref, cost, cons, dual, limit, agreed, acc, k_top, k_bot, r_top, r_bot,
    pack, unpack, sent, got, gen_sent, gen_got,
    in_sems, out_sems, tie_send, tie_recv, gen_send, gen_recv,
):
    slots, hours = cost.shape
    pair_lines = ties // (areas - 1)
    pad_lines = sent.shape[2]
    split = k_top.shape[1] // 3
    head = GENS + round_up(ties, 16)
    tie_rows = head - GENS
    me = lax.axis_index("area")
    mine = lax.axis_index("ctg")

    barrier = pltpu.get_barrier_semaphore()
    step = round_up(-(-(slots - head) // 3), 16)
    chunks = [(0, head)] + [(a, min(a + step, slots)) for a in range(head, slots, step)]

    def load(src, dst, index):
        return pltpu.make_async_copy(src, dst, in_sems.at[index])

    loads = [
        load(cons_hbm.at[0, 0], cons, 0),
        load(dual_hbm.at[0, 0], dual, 1),
        load(cost_hbm.at[0, 0], cost, 2),
    ]
    k_loads = [
        load(k_hbm.at[0, 0, pl.ds(a, b - a)], k_ref.at[pl.ds(a, b - a)], 4 + j)
        for j, (a, b) in enumerate(chunks)
    ]
    limit_load = load(limit_hbm.at[0], limit, 3)
    for copy in loads:
        copy.start()
    for copy in k_loads:
        copy.start()
    limit_load.start()

    def each_peer(body):
        if areas <= 8:
            for o in range(areas - 1):
                body(o)
        else:
            lax.fori_loop(0, areas - 1, lambda o, c: (body(o), c)[1], 0)

    def greet(o):
        pl.semaphore_signal(
            barrier, inc=1, device_id={"area": lax.rem(me + o + 1, areas)}, device_id_type=MESH
        )

    each_peer(greet)
    for o in range(1, scenarios):
        pl.semaphore_signal(
            barrier, inc=1, device_id={"ctg": lax.rem(mine + o, scenarios)}, device_id_type=MESH
        )

    size = size_ref[0]

    def live_rows(a, b):
        return lax.broadcasted_iota(jnp.int32, (b - a, hours), 0) + a < size

    peers = jnp.concatenate(
        [peer_ref[...], jnp.full((1, tie_rows - ties), -1, jnp.int32)], axis=1
    ) if tie_rows > ties else peer_ref[...]
    row_id = lax.broadcasted_iota(jnp.int32, (tie_rows, tie_rows), 0)
    col_id = lax.broadcasted_iota(jnp.int32, (tie_rows, tie_rows), 1)
    across = jnp.broadcast_to(peers, (tie_rows, tie_rows))
    down = jnp.sum(jnp.where(row_id == col_id, across, 0), axis=1, keepdims=True)
    same = across == down
    rank_row = jnp.sum(jnp.where(same & (row_id < col_id), 1, 0), axis=0, keepdims=True)
    rank_col = jnp.sum(jnp.where(same & (col_id < row_id), 1, 0), axis=1, keepdims=True)

    def place(peer, rank):
        back = peer - me - 1
        turn = jnp.where(back < 0, back + areas, back)
        return jnp.where(peer < 0, -1, turn * pad_lines + rank)

    lanes = areas * pad_lines
    dest_row = place(peers, rank_row)
    dest_col = place(down, rank_col)
    pack[...] = jnp.where(
        lax.broadcasted_iota(jnp.int32, (lanes, tie_rows), 0) == dest_row, 1.0, 0.0
    ).astype(jnp.bfloat16)
    unpack[...] = jnp.where(
        lax.broadcasted_iota(jnp.int32, (tie_rows, lanes), 1) == dest_col, 1.0, 0.0
    ).astype(jnp.bfloat16)
    for it in range(ITERS):
        got[it, areas - 1] = jnp.zeros((pad_lines, hours), jnp.float32)

    def put_right(side, a, b, value):
        high, low = split_two(value)
        for lo, hi, ref in ((0, split, r_top), (split, slots, r_bot)):
            first, last = max(a, lo), min(b, hi)
            if first < last:
                span = hi - lo
                for j, part in enumerate((high, high, low)):
                    ref[side, j * span + first - lo:j * span + last - lo] = part[first - a:last - a]

    def convert(a, b):
        def body(g, carry):
            row = pl.multiple_of(a + g * 16, 16)
            first = pl.multiple_of(row // 128 * 128, 128)
            where = (pl.ds(row, 16), pl.ds(first, 128))
            on = lax.broadcasted_iota(jnp.int32, (16, 128), 0) + row == (
                lax.broadcasted_iota(jnp.int32, (16, 128), 1) + first
            )
            k_ref[where] = k_ref[where] + jnp.where(on, diag_ref[0, :, pl.ds(first, 128)], 0.0)
            high, low = split_two(k_ref[pl.ds(row, 16), :])
            for lo, hi, ref in ((0, split, k_top), (split, slots, k_bot)):
                span = hi - lo
                ref[pl.ds(row, 16), :span] = high[:, lo:hi]
                ref[pl.ds(row, 16), span:2 * span] = low[:, lo:hi]
                ref[pl.ds(row, 16), 2 * span:] = high[:, lo:hi]
            return carry

        lax.fori_loop(0, (b - a) // 16, body, 0)

    def product_of(it, a, b):
        near = fast_dot(k_top[a:b], r_top[it % 2])
        return near + (fast_dot(k_bot[a:b], r_bot[0]) if it == 0 else acc[a:b])

    def update(it, a, b, averaged, shifted):
        clipped = jnp.clip(averaged, -limit[a:b], limit[a:b])
        rest = shifted - clipped
        dual[a:b] = rest
        if it == ITERS - 1:
            agreed[a:b] = clipped
        else:
            put_right((it + 1) % 2, a, b, clipped - rest - cost[a:b])

    def tie_copy(it, o):
        return pltpu.make_async_remote_copy(
            src_ref=sent.at[it, o], dst_ref=got.at[it, areas - 2 - o],
            send_sem=tie_send.at[it], recv_sem=tie_recv.at[it],
            device_id={"area": lax.rem(me + o + 1, areas)}, device_id_type=MESH,
        )

    def tie_all(it):
        return pltpu.make_async_remote_copy(
            src_ref=sent.at[it, pl.ds(0, areas - 1)], dst_ref=got.at[it, pl.ds(0, areas - 1)],
            send_sem=tie_send.at[it], recv_sem=tie_recv.at[it],
            device_id={"area": lax.rem(me + 1, areas)}, device_id_type=MESH,
        )

    def gen_copy(it, o):
        return pltpu.make_async_remote_copy(
            src_ref=gen_sent.at[it], dst_ref=gen_got.at[it, o - 1],
            send_sem=gen_send.at[it, o - 1], recv_sem=gen_recv.at[it, o - 1],
            device_id={"ctg": lax.rem(mine + o, scenarios)}, device_id_type=MESH,
        )

    def send_ties(it, shifted):
        sent[it] = move_rows(pack[...], shifted).reshape(areas, pad_lines, hours)
        each_peer(lambda o: tie_copy(it, o).start())

    def out_copies(a, b, index):
        where = pl.ds(a, b - a)
        return [
            pltpu.make_async_copy(agreed.at[where], agreed_hbm.at[0, 0, where], out_sems.at[0, index]),
            pltpu.make_async_copy(dual.at[where], dualout_hbm.at[0, 0, where], out_sems.at[1, index]),
        ]

    for copy in loads:
        copy.wait()
    for a in range(0, slots, 128):
        b = min(a + 128, slots)
        live = live_rows(a, b)
        linear = jnp.where(live, cost[a:b], 0.0)
        cost[a:b] = linear
        put_right(0, a, b, jnp.where(live, cons[a:b] - dual[a:b], 0.0) - linear)

    for it in range(ITERS):
        last = it == ITERS - 1
        if it == 0:
            k_loads[0].wait()
            convert(0, head)
        for a, b in ((GENS, head), (0, GENS)):
            product = product_of(it, a, b)
            shifted = jnp.where(live_rows(a, b), product + dual[a:b], 0.0)
            if a == GENS:
                acc[a:b] = shifted
                if it == 0:
                    pl.semaphore_wait(barrier, areas - 1 + scenarios - 1)
                send_ties(it, shifted)
            else:
                gen_sent[it] = shifted
                for o in range(1, scenarios):
                    gen_copy(it, o).start()
        if it == 0:
            limit_load.wait()
        for j, (a, b) in enumerate(chunks[1:]):
            if it == 0:
                k_loads[j + 1].wait()
                convert(a, b)
            product = product_of(it, a, b)
            shifted = jnp.where(live_rows(a, b), product + dual[a:b], 0.0)
            update(it, a, b, shifted, shifted)
            if last:
                for copy in out_copies(a, b, j + 1):
                    copy.start()
        tie_shifted = acc[GENS:head]
        if not last:
            for a, b in chunks:
                acc[a:b] = fast_dot(k_bot[a:b], r_bot[(it + 1) % 2])
        for o in range(1, scenarios):
            gen_copy(it, o).wait_recv()
        own = gen_sent[it]
        total = own
        for o in range(1, scenarios):
            total = total + gen_got[it, o - 1]
        update(it, 0, GENS, total * (1.0 / scenarios), own)
        tie_all(it).wait_recv()
        other = move_rows(unpack[...], got[it].reshape(lanes, hours))
        is_tie = lax.broadcasted_iota(jnp.int32, (tie_rows, hours), 0) < ties
        averaged = jnp.where(is_tie, 0.5 * (tie_shifted + other), tie_shifted)
        update(it, GENS, head, averaged, tie_shifted)

    for copy in out_copies(0, head, 0):
        copy.start()
    for it in range(ITERS):
        tie_all(it).wait_send()
        for o in range(1, scenarios):
            gen_copy(it, o).wait_send()
    for j, (a, b) in enumerate(chunks):
        for copy in out_copies(a, b, j):
            copy.wait()


def local(area_size, tie_peer, kkt_diag, kkt_offdiag, cost, consensus, dual, limit):
    areas = lax.axis_size("area")
    scenarios = lax.axis_size("ctg")
    ties = tie_peer.shape[1]
    slots, hours = cost.shape[2:]
    pad_lines = round_up(ties // (areas - 1), 8)
    tie_rows = round_up(ties, 16)
    split = round_up(GENS + tie_rows, 256)
    f32, b16 = jnp.float32, jnp.bfloat16
    vmem = pltpu.VMEM
    whole = pl.BlockSpec(memory_space=vmem)
    far = pl.BlockSpec(memory_space=pltpu.HBM)
    dma = pltpu.SemaphoreType.DMA
    out = jax.ShapeDtypeStruct(cost.shape, f32)
    lanes = areas * pad_lines
    state = vmem((slots, hours), f32)
    return pl.pallas_call(
        functools.partial(kernel, areas, scenarios, ties),
        out_shape=(out, out),
        in_specs=[pl.BlockSpec(memory_space=pltpu.SMEM), whole, whole, far, far, far, far, far],
        out_specs=(far, far),
        scratch_shapes=[
            vmem((slots, slots), f32), state, state, state, state, state, state,
            vmem((slots, 3 * split), b16), vmem((slots, 3 * (slots - split)), b16),
            vmem((2, 3 * split, hours), b16), vmem((2, 3 * (slots - split), hours), b16),
            vmem((lanes, tie_rows), b16), vmem((tie_rows, lanes), b16),
            vmem((ITERS, areas, pad_lines, hours), f32),
            vmem((ITERS, areas, pad_lines, hours), f32),
            vmem((ITERS, GENS, hours), f32),
            vmem((ITERS, scenarios - 1, GENS, hours), f32),
            dma((8,)), dma((2, 4)), dma((ITERS,)), dma((ITERS,)),
            dma((ITERS, scenarios - 1)), dma((ITERS, scenarios - 1)),
        ],
        compiler_params=pltpu.CompilerParams(
            collective_id=0, has_side_effects=True, vmem_limit_bytes=48 * 1024 * 1024
        ),
    )(area_size, tie_peer, kkt_diag, kkt_offdiag, cost, consensus, dual, limit)


def solution(mesh):
    return jax.shard_map(
        local,
        mesh=mesh,
        in_specs=(
            P(("grp", "area")),
            P(("grp", "area"), None),
            P(("grp", "area"), "ctg", None),
            P(("grp", "area"), "ctg", None, None),
            P(("grp", "area"), "ctg", None, None),
            P(("grp", "area"), "ctg", None, None),
            P(("grp", "area"), "ctg", None, None),
            P(("grp", "area"), None, None),
        ),
        out_specs=(P(("grp", "area"), "ctg", None, None), P(("grp", "area"), "ctg", None, None)),
        check_vma=False,
    )
```

time: 140 us -> 31.2 us (0.22)
  waiting for transfers between devices: 33.7 us -> 0 us
  starting transfers between devices: 32.4 us -> 0 us
  Pallas kernels: 0 us -> 22.7 us
  matrix products: 19.8 us -> 0 us
  other arithmetic: 19.3 us -> 0 us
  between operations: 14.6 us -> 1.3 us
  local copies, waits for them, and re-layouts: 18.8 us -> 6.95 us
    all_to_all x6 -> x0, starting transfers between devices: 32.3 us -> none  [the longest x3 17.5 us: local(): lax.all_to_all(sent_primal, 'area', split_axis=0, concat_axis=0, tiled=True)]
    pallas_call x0 -> x1, Pallas kernels: none -> 22.7 us  [local(): pl.pallas_call(functools.partial(kernel, areas, scenarios, ties), out_sha...]
    all_to_all x6 -> x0, waiting for transfers between devices: 22.6 us -> none  [the longest x3 14.8 us: local(): lax.all_to_all(sent_primal, 'area', split_axis=0, concat_axis=0, tiled=True)]
    dot_general x3 -> x0, matrix products: 19.8 us -> none  [apply_rows(): jnp.dot(matrix, right_side, precision=lax.Precision.HIGHEST, preferred_el...]
    psum x3 -> x0, waiting for transfers between devices: 11.1 us -> none  [local(): gen_mean = lax.psum(shifted[:GENS], 'ctg') / scenarios]
    mul x6 -> x0, other arithmetic: 6.56 us -> none  [the longest x2 4.41 us: local(): dual_var = live * (dual_var + primal - agreed)]
    unnamed x16 -> x12, local copies, waits for them, and re-layouts: 1 us -> 6.95 us
    all_to_all x12 -> x0, local copies, waits for them, and re-layouts: 5.53 us -> none  [the longest x6 2.78 us: local(): lax.all_to_all(sent_primal, 'area', split_axis=0, concat_axis=0, tiled=True)]
  transfers between devices with their start and end apart: 9 -> 0, of which waited for: 8 -> 0; matrix products, arithmetic and copies ran while one was open for 17% -> 0% of each run, Pallas kernels for 0% -> 0%
where the time goes in v1:
time: 31.2 us; the launch traced here: 30.9 us
  Pallas kernels  22.7 us (73%)
  local copies, waits for them, and re-layouts  6.95 us (22%)
  between operations  1.3 us (4%)
    pallas_call x1, Pallas kernels, local(): pl.pallas_call(functools.partial(kernel, areas, scenarios, ties), out_sha...  22.7 us
    unnamed x12, local copies, waits for them, and re-layouts  6.95 us

profile of v1, /device:TPU:0, one launch (start us, length us, event | category | flops | bytes accessed | tf_op | source)
XLA Modules:
  0.0 30.9 jit_solution(16152051783268382960)
XLA Ops:
  1.3 0.0 copy-start
  1.3 1.2 %copy-done = f32[1,1,1024,256]{3,2,1,0:T(8,128)S(1)} copy-done((f32[1,1,1024,256]{3,2,1,0:T(8,128)S(1)}, f32[1,1,1024,256]{3,2,1,0:T(8,128)}, u32[]{:S(2)}) %copy-start) | copy-done | bytes 1048600
  2.5 0.0 copy-start.1
  2.5 1.2 %copy-done.1 = f32[1,1,1024,256]{3,2,1,0:T(8,128)S(1)} copy-done((f32[1,1,1024,256]{3,2,1,0:T(8,128)S(1)}, f32[1,1,1024,256]{3,2,1,0:T(8,128)}, u32[]{:S(2)}) %copy-start.1) | copy-done | bytes 1048600
  3.7 0.0 copy-start.2
  3.7 1.2 %copy-done.2 = f32[1,1,1024,256]{3,2,1,0:T(8,128)S(1)} copy-done((f32[1,1,1024,256]{3,2,1,0:T(8,128)S(1)}, f32[1,1,1024,256]{3,2,1,0:T(8,128)}, u32[]{:S(2)}) %copy-start.2) | copy-done | bytes 1048600
  5.0 0.0 copy-start.3
  5.0 0.7 %copy-done.3 = f32[1,1,1024]{2,1,0:T(1,128)S(1)} copy-done((f32[1,1,1024]{2,1,0:T(1,128)S(1)}, f32[1,1,1024]{2,1,0:T(1,128)}, u32[]{:S(2)}) %copy-start.3) | copy-done | bytes 4120
  5.6 0.0 copy-start.4
  5.6 0.7 %copy-done.4 = s32[1,42]{1,0:T(1,128)S(1)} copy-done((s32[1,42]{1,0:T(1,128)S(1)}, s32[1,42]{1,0:T(1,128)}, u32[]{:S(2)}) %copy-start.4) | copy-done | bytes 192
  6.3 22.7 %shard_map.95 = (f32[1,1,1024,256]{3,2,1,0:T(8,128)S(1)}, f32[1,1,1024,256]{3,2,1,0:T(8,128)S(1)}) custom-call(s32[1]{0:T(128)S(6)} %copy.12.size_ref, s32[1,42]{1,0:T(1,128)S(1)} %copy-done.4, f32[1,1,1024]{2,1,0:T(1,128)S(1)} %copy-done.3, f32[1,1,1024,1024]{3,2,1,0:T(8,128)} %k_hbm.1, f32[1,1,1024,256]{3,2,1,0:T(8,128)S(1)} %copy-done, ...), custom_call_target="tpu_custom_call" | custom-call | tf_op jit(solution)/shard_map/pallas_call | solution.py:284
  29.0 1.0 %copy.13 = f32[1,1,1024,256]{3,2,1,0:T(8,128)} copy(f32[1,1,1024,256]{3,2,1,0:T(8,128)S(1)} %get-tuple-element.4) | data formatting | bytes 2097152
  29.9 1.0 %copy.14 = f32[1,1,1024,256]{3,2,1,0:T(8,128)} copy(f32[1,1,1024,256]{3,2,1,0:T(8,128)S(1)} %get-tuple-element.5) | data formatting | bytes 2097152
Async XLA Ops:
  1.3 1.2 %copy-start = (f32[1,1,1024,256]{3,2,1,0:T(8,128)S(1)}, f32[1,1,1024,256]{3,2,1,0:T(8,128)}, u32[]{:S(2)}) copy-start(f32[1,1,1024,256]{3,2,1,0:T(8,128)} %cost_hbm.1) | copy-start | bytes 3145732
  2.5 1.2 %copy-start.1 = (f32[1,1,1024,256]{3,2,1,0:T(8,128)S(1)}, f32[1,1,1024,256]{3,2,1,0:T(8,128)}, u32[]{:S(2)}) copy-start(f32[1,1,1024,256]{3,2,1,0:T(8,128)} %cons_hbm.1) | copy-start | bytes 3145732
  3.7 1.2 %copy-start.2 = (f32[1,1,1024,256]{3,2,1,0:T(8,128)S(1)}, f32[1,1,1024,256]{3,2,1,0:T(8,128)}, u32[]{:S(2)}) copy-start(f32[1,1,1024,256]{3,2,1,0:T(8,128)} %dual_hbm.1) | copy-start | bytes 3145732
  5.0 0.7 %copy-start.3 = (f32[1,1,1024]{2,1,0:T(1,128)S(1)}, f32[1,1,1024]{2,1,0:T(1,128)}, u32[]{:S(2)}) copy-start(f32[1,1,1024]{2,1,0:T(1,128)} %diag_ref.1) | copy-start | bytes 12292
  5.6 0.7 %copy-start.4 = (s32[1,42]{1,0:T(1,128)S(1)}, s32[1,42]{1,0:T(1,128)}, u32[]{:S(2)}) copy-start(s32[1,42]{1,0:T(1,128)} %peer_ref.1) | copy-start | bytes 508

commit v2 on v1

--- a/solution.py
+++ b/solution.py
@@ -37,11 +37,11 @@
 
 
 def kernel(
-    areas, scenarios, ties, size_ref, peer_ref, diag_ref, k_hbm, cost_hbm, cons_hbm, dual_hbm,
-    limit_hbm, agreed_hbm, dualout_hbm,
-    k_ref, cost, cons, dual, limit, agreed, acc, k_top, k_bot, r_top, r_bot,
+    areas, scenarios, ties, size_hbm, peer_hbm, diag_hbm, k_hbm, cost_hbm, cons_hbm, dual_hbm,
+    limit_hbm, agreed_out, dual_out,
+    size_ref, peer_ref, diag_ref, k_ref, cost, cons, dual, limit, acc, k_top, k_bot, r_top, r_bot,
     pack, unpack, sent, got, gen_sent, gen_got,
-    in_sems, out_sems, tie_send, tie_recv, gen_send, gen_recv,
+    in_sems, tie_send, tie_recv, gen_send, gen_recv,
 ):
     slots, hours = cost.shape
     pair_lines = ties // (areas - 1)
@@ -59,17 +59,22 @@
     def load(src, dst, index):
         return pltpu.make_async_copy(src, dst, in_sems.at[index])
 
+    small_loads = [
+        load(size_hbm, size_ref, 3),
+        load(peer_hbm, peer_ref, 4),
+        load(diag_hbm, diag_ref, 5),
+    ]
     loads = [
         load(cons_hbm.at[0, 0], cons, 0),
         load(dual_hbm.at[0, 0], dual, 1),
         load(cost_hbm.at[0, 0], cost, 2),
     ]
     k_loads = [
-        load(k_hbm.at[0, 0, pl.ds(a, b - a)], k_ref.at[pl.ds(a, b - a)], 4 + j)
+        load(k_hbm.at[0, 0, pl.ds(a, b - a)], k_ref.at[pl.ds(a, b - a)], 7 + j)
         for j, (a, b) in enumerate(chunks)
     ]
-    limit_load = load(limit_hbm.at[0], limit, 3)
-    for copy in loads:
+    limit_load = load(limit_hbm.at[0], limit, 6)
+    for copy in small_loads + loads:
         copy.start()
     for copy in k_loads:
         copy.start()
@@ -93,6 +98,8 @@
             barrier, inc=1, device_id={"ctg": lax.rem(mine + o, scenarios)}, device_id_type=MESH
         )
 
+    for copy in small_loads:
+        copy.wait()
     size = size_ref[0]
 
     def live_rows(a, b):
@@ -136,8 +143,16 @@
                     ref[side, j * span + first - lo:j * span + last - lo] = part[first - a:last - a]
 
     def convert(a, b):
+        groups = (b - a) // 16
+        batch = max(m for m in (1, 2, 3, 4, 5) if groups % m == 0)
+
         def body(g, carry):
-            row = pl.multiple_of(a + g * 16, 16)
+            for m in range(batch):
+                rows_of(a + (g * batch + m) * 16)
+            return carry
+
+        def rows_of(row):
+            row = pl.multiple_of(row, 16)
             first = pl.multiple_of(row // 128 * 128, 128)
             where = (pl.ds(row, 16), pl.ds(first, 128))
             on = lax.broadcasted_iota(jnp.int32, (16, 128), 0) + row == (
@@ -150,9 +165,8 @@
                 ref[pl.ds(row, 16), :span] = high[:, lo:hi]
                 ref[pl.ds(row, 16), span:2 * span] = low[:, lo:hi]
                 ref[pl.ds(row, 16), 2 * span:] = high[:, lo:hi]
-            return carry
-
-        lax.fori_loop(0, (b - a) // 16, body, 0)
+
+        lax.fori_loop(0, groups // batch, body, 0)
 
     def product_of(it, a, b):
         near = fast_dot(k_top[a:b], r_top[it % 2])
@@ -161,10 +175,11 @@
     def update(it, a, b, averaged, shifted):
         clipped = jnp.clip(averaged, -limit[a:b], limit[a:b])
         rest = shifted - clipped
-        dual[a:b] = rest
         if it == ITERS - 1:
-            agreed[a:b] = clipped
+            agreed_out[0, 0, a:b] = clipped
+            dual_out[0, 0, a:b] = rest
         else:
+            dual[a:b] = rest
             put_right((it + 1) % 2, a, b, clipped - rest - cost[a:b])
 
     def tie_copy(it, o):
@@ -191,13 +206,6 @@
     def send_ties(it, shifted):
         sent[it] = move_rows(pack[...], shifted).reshape(areas, pad_lines, hours)
         each_peer(lambda o: tie_copy(it, o).start())
-
-    def out_copies(a, b, index):
-        where = pl.ds(a, b - a)
-        return [
-            pltpu.make_async_copy(agreed.at[where], agreed_hbm.at[0, 0, where], out_sems.at[0, index]),
-            pltpu.make_async_copy(dual.at[where], dualout_hbm.at[0, 0, where], out_sems.at[1, index]),
-        ]
 
     for copy in loads:
         copy.wait()
@@ -212,7 +220,8 @@
         last = it == ITERS - 1
         if it == 0:
             k_loads[0].wait()
-            convert(0, head)
+            convert(GENS, head)
+            convert(0, GENS)
         for a, b in ((GENS, head), (0, GENS)):
             product = product_of(it, a, b)
             shifted = jnp.where(live_rows(a, b), product + dual[a:b], 0.0)
@@ -234,9 +243,6 @@
             product = product_of(it, a, b)
             shifted = jnp.where(live_rows(a, b), product + dual[a:b], 0.0)
             update(it, a, b, shifted, shifted)
-            if last:
-                for copy in out_copies(a, b, j + 1):
-                    copy.start()
         tie_shifted = acc[GENS:head]
         if not last:
             for a, b in chunks:
@@ -254,15 +260,24 @@
         averaged = jnp.where(is_tie, 0.5 * (tie_shifted + other), tie_shifted)
         update(it, GENS, head, averaged, tie_shifted)
 
-    for copy in out_copies(0, head, 0):
-        copy.start()
     for it in range(ITERS):
         tie_all(it).wait_send()
         for o in range(1, scenarios):
             gen_copy(it, o).wait_send()
-    for j, (a, b) in enumerate(chunks):
-        for copy in out_copies(a, b, j):
-            copy.wait()
+
+def flush(agreed, dual, agreed_hbm, dual_hbm, sems):
+    slots = agreed.shape[2]
+    pieces = 4
+    step = slots // pieces
+    copies = []
+    for j in range(pieces):
+        where = (0, 0, pl.ds(j * step, step))
+        copies.append(pltpu.make_async_copy(agreed.at[where], agreed_hbm.at[where], sems.at[0, j]))
+        copies.append(pltpu.make_async_copy(dual.at[where], dual_hbm.at[where], sems.at[1, j]))
+    for copy in copies:
+        copy.start()
+    for copy in copies:
+        copy.wait()
 
 
 def local(area_size, tie_peer, kkt_diag, kkt_offdiag, cost, consensus, dual, limit):
@@ -275,19 +290,20 @@
     split = round_up(GENS + tie_rows, 256)
     f32, b16 = jnp.float32, jnp.bfloat16
     vmem = pltpu.VMEM
-    whole = pl.BlockSpec(memory_space=vmem)
     far = pl.BlockSpec(memory_space=pltpu.HBM)
     dma = pltpu.SemaphoreType.DMA
     out = jax.ShapeDtypeStruct(cost.shape, f32)
+    near = pltpu.VMEM(cost.shape, f32)
     lanes = areas * pad_lines
     state = vmem((slots, hours), f32)
-    return pl.pallas_call(
+    agreed, dual_var = pl.pallas_call(
         functools.partial(kernel, areas, scenarios, ties),
-        out_shape=(out, out),
-        in_specs=[pl.BlockSpec(memory_space=pltpu.SMEM), whole, whole, far, far, far, far, far],
-        out_specs=(far, far),
+        out_shape=(near, near),
+        in_specs=[far] * 8,
+        out_specs=(pl.BlockSpec(memory_space=vmem),) * 2,
         scratch_shapes=[
-            vmem((slots, slots), f32), state, state, state, state, state, state,
+            pltpu.SMEM((1,), jnp.int32), vmem(tie_peer.shape, jnp.int32), vmem(kkt_diag.shape, f32),
+            vmem((slots, slots), f32), state, state, state, state, state,
             vmem((slots, 3 * split), b16), vmem((slots, 3 * (slots - split)), b16),
             vmem((2, 3 * split, hours), b16), vmem((2, 3 * (slots - split), hours), b16),
             vmem((lanes, tie_rows), b16), vmem((tie_rows, lanes), b16),
@@ -295,13 +311,21 @@
             vmem((ITERS, areas, pad_lines, hours), f32),
             vmem((ITERS, GENS, hours), f32),
             vmem((ITERS, scenarios - 1, GENS, hours), f32),
-            dma((8,)), dma((2, 4)), dma((ITERS,)), dma((ITERS,)),
+            dma((11,)), dma((ITERS,)), dma((ITERS,)),
             dma((ITERS, scenarios - 1)), dma((ITERS, scenarios - 1)),
         ],
         compiler_params=pltpu.CompilerParams(
-            collective_id=0, has_side_effects=True, vmem_limit_bytes=48 * 1024 * 1024
+            collective_id=0, has_side_effects=True, vmem_limit_bytes=60 * 1024 * 1024
         ),
     )(area_size, tie_peer, kkt_diag, kkt_offdiag, cost, consensus, dual, limit)
+    anywhere = pl.BlockSpec(memory_space=vmem)
+    return pl.pallas_call(
+        flush,
+        out_shape=(out, out),
+        in_specs=[anywhere] * 2,
+        out_specs=(far, far),
+        scratch_shapes=[dma((2, 4))],
+    )(*[pltpu.with_memory_space_constraint(x, pltpu.VMEM) for x in (agreed, dual_var)])
 
 
 def solution(mesh):

time: 31.2 us -> 24.8 us (0.79)
  local copies, waits for them, and re-layouts: 6.95 us -> 0 us
  Pallas kernels: 22.7 us -> 23.3 us
    unnamed x12 -> x0, local copies, waits for them, and re-layouts: 6.95 us -> none
    pallas_call x0 -> x1, Pallas kernels: none -> 1.38 us  [local(): pl.pallas_call(flush, out_shape=(out, out), in_specs=[anywhere] * 2, out_...]
    pallas_call x1, Pallas kernels: 22.7 us -> 22 us  [local(): pl.pallas_call(functools.partial(kernel, areas, scenarios, ties), out_sha...]
where the time goes in v2:
time: 24.8 us; the launch traced here: 24.6 us
  Pallas kernels  23.3 us (94%)
  between operations  1.29 us (5%)
    pallas_call x1, Pallas kernels, local(): pl.pallas_call(functools.partial(kernel, areas, scenarios, ties), out_sha...  22 us
    pallas_call x1, Pallas kernels, local(): pl.pallas_call(flush, out_shape=(out, out), in_specs=[anywhere] * 2, out_...  1.38 us

profile of v2, /device:TPU:0, one launch (start us, length us, event | category | flops | bytes accessed | tf_op | source)
XLA Modules:
  0.0 24.6 jit_solution(17190231588502288875)
XLA Ops:
  1.3 22.0 %shard_map.95 = (f32[1,1,1024,256]{3,2,1,0:T(8,128)S(1)}, f32[1,1,1024,256]{3,2,1,0:T(8,128)S(1)}) custom-call(s32[1]{0:T(128)S(6)} %copy.10.size_hbm, s32[1,42]{1,0:T(1,128)} %peer_hbm.1, f32[1,1,1024]{2,1,0:T(1,128)} %diag_hbm.1, f32[1,1,1024,1024]{3,2,1,0:T(8,128)} %k_hbm.1, f32[1,1,1024,256]{3,2,1,0:T(8,128)} %cost_hbm.1, f32[1,1,1024,256]{3,2,1,0:T(8,128)} %cons_hbm.1, ...), custom_call_target="tpu_custom_call" | custom-call | tf_op jit(solution)/shard_map/pallas_call | solution.py:299
  23.3 1.4 %shard_map.96 = (f32[1,1,1024,256]{3,2,1,0:T(8,128)}, f32[1,1,1024,256]{3,2,1,0:T(8,128)}) custom-call(f32[1,1,1024,256]{3,2,1,0:T(8,128)S(1)} %get-tuple-element.4.agreed, f32[1,1,1024,256]{3,2,1,0:T(8,128)S(1)} %get-tuple-element.5.dual), custom_call_target="tpu_custom_call" | custom-call | tf_op jit(solution)/shard_map/pallas_call | solution.py:322
